TPU v7x, 32 devices: a whole 2x2x4 slice. The times are simulated.
32 devices in a mesh: groups: 2 (over y), seq: 16 (over z, x, core).
Axes of the slice: x: 2, y: 2, z: 4, core: 2. Of those that a mesh axis runs over, the one named last changes fastest.
Arguments:
- queries: bfloat16 [8192, 4096], P(('groups', 'seq')), parts along dimension 0, may hold values from -6 to 6
- stretch_keys: bfloat16 [8192, 1024], P(('groups', 'seq')), parts along dimension 0, may hold values from -4 to 4
- prefill_values: bfloat16 [8192, 1024], P(('groups', 'seq')), parts along dimension 0, may hold values from -6 to 6
- earlier_keys: bfloat16 [16384, 1024], P(('groups', 'seq')), parts along dimension 0, may hold values from -6 to 6
- earlier_values: bfloat16 [16384, 1024], P(('groups', 'seq')), parts along dimension 0, may hold values from -6 to 6
- selected: int32 [16, 3], P('groups'), parts along dimension 0, may hold values from 0 to 15, all different within a row
Outputs:
- attended: bfloat16 [8192, 4096], P(('groups', 'seq')), parts along dimension 0
There are 2 independent parts, one for each index of `groups`. A program takes and returns all parts, laid end to end along the dimension named above; each array names one. Nothing has to cross between parts.
Inputs may be any that keep to these rules, and one draw needn't show every extreme that they name: `selected`: each row names 3 different cache blocks, and every cache block is named by some row.
All inputs are finite; a program needn't handle non-finite values.
Results may differ from a plain program's by a relative error of at most 0.008.
Values may be sent and summed in bfloat16 or wider, within the bound.
A program may use at most 128 MiB of HBM per device.

v0:
```python
import jax
import jax.numpy as jnp
from jax import lax
from jax.sharding import PartitionSpec as P

QUERY_HEADS = 32
KEY_VALUE_HEADS = 8
HEAD_SIZE = 128
BLK = 512
TOPK = 3


def passed_along(block, axis, distance):
    devices = range(lax.axis_size(axis))
    route = [(i - distance, i) for i in devices if i - distance in devices]
    return lax.ppermute(block, axis, route)


def attend_local(rows_of_queries, rows_of_keys, rows_of_values, allowed):
    count_of_rows = rows_of_queries.shape[0]
    count_of_keys = rows_of_keys.shape[0]
    group_width = QUERY_HEADS // KEY_VALUE_HEADS
    heads_of_queries = jnp.moveaxis(
        rows_of_queries.reshape(count_of_rows, KEY_VALUE_HEADS, group_width, HEAD_SIZE), 1, 0
    )
    heads_of_keys = jnp.moveaxis(
        rows_of_keys.reshape(count_of_keys, KEY_VALUE_HEADS, HEAD_SIZE), 1, 0
    )
    heads_of_values = jnp.moveaxis(
        rows_of_values.reshape(count_of_keys, KEY_VALUE_HEADS, HEAD_SIZE), 1, 0
    )

    def one_head(operands):
        head_queries, head_keys, head_values = operands
        scores = jnp.einsum(
            "rgd,kd->grk", head_queries, head_keys, preferred_element_type=jnp.float32
        ) * HEAD_SIZE ** (-0.5)
        scores = jnp.where(allowed[None], scores, -1e30)
        largest = jnp.max(scores, axis=-1, keepdims=True)
        expon = jnp.exp(scores - largest)
        weights = (expon / jnp.sum(expon, axis=-1, keepdims=True)).astype(jnp.bfloat16)
        result = jnp.einsum("grk,kd->rgd", weights, head_values, preferred_element_type=jnp.float32)
        return result.astype(jnp.bfloat16)

    outputs = lax.map(one_head, (heads_of_queries, heads_of_keys, heads_of_values))
    return jnp.moveaxis(outputs, 0, 1).reshape(count_of_rows, QUERY_HEADS * HEAD_SIZE)


def per_device(queries, stretch_keys, prefill_values, earlier_keys, earlier_values, selected):
    members = lax.axis_size("seq")
    position = lax.axis_index("seq")
    query_count = queries.shape[0]
    key_value_width = stretch_keys.shape[1]
    cache_blocks = earlier_keys.shape[0] // BLK
    piece_rows = BLK // members
    stacked = jnp.stack([earlier_keys, earlier_values]).reshape(
        2, cache_blocks, members, piece_rows, key_value_width
    )
    spread = lax.all_to_all(stacked, "seq", split_axis=2, concat_axis=1, tiled=True)
    pieces = spread.reshape(2, cache_blocks * members, piece_rows, key_value_width)
    span = BLK // query_count
    owner_block = jnp.arange(members, dtype=jnp.int32) // span
    wanted = selected[owner_block]
    outgoing = pieces[:, wanted]
    incoming = lax.all_to_all(outgoing, "seq", split_axis=1, concat_axis=1, tiled=True)
    picked = jnp.transpose(incoming, (0, 2, 1, 3, 4)).reshape(2, TOPK * BLK, key_value_width)
    local_pair = jnp.stack([stretch_keys, prefill_values])
    earlier = [passed_along(local_pair, "seq", 1)]
    own_pair = jnp.concatenate(earlier + [local_pair], axis=1)
    place = position % span
    query_pos = place * query_count + jnp.arange(query_count, dtype=jnp.int32)
    key_pos = jnp.arange(BLK, dtype=jnp.int32) - (span - 1 - place) * query_count
    allowed_own = (key_pos[None, :] >= 0) & (key_pos[None, :] <= query_pos[:, None])
    allowed = jnp.concatenate(
        [jnp.ones((query_count, TOPK * BLK), dtype=bool), allowed_own], axis=1
    )
    rows_of_keys = jnp.concatenate([picked[0], own_pair[0]], axis=0)
    rows_of_values = jnp.concatenate([picked[1], own_pair[1]], axis=0)
    return attend_local(queries, rows_of_keys, rows_of_values, allowed)


def solution(mesh):
    return jax.shard_map(
        per_device,
        mesh=mesh,
        in_specs=(
            P(("groups", "seq"), None),
            P(("groups", "seq"), None),
            P(("groups", "seq"), None),
            P(("groups", "seq"), None),
            P(("groups", "seq"), None),
            P("groups", None),
        ),
        out_specs=P(("groups", "seq"), None),
        check_vma=False,
    )
```

profile of v0, /device:TPU:16, one launch (start us, length us, event | category | flops | bytes accessed | tf_op | source)
XLA Modules:
  0.0 355.8 jit_solution(1939000373582190951)
XLA Ops:
  3.1 6.2 %all-to-all-start = ((bf16[2,1,16,32,1024]{4,3,1,0,2:T(8,128)(2,1)}), bf16[2,1,16,32,1024]{4,3,1,0,2:T(8,128)(2,1)S(1)}, u32[]{:S(2)}, u32[]{:S(2)}) async-start(bf16[2,1,16,32,1024]{4,3,1,0,2:T(8,128)(2,1)} %pad_maximum_fusion), calls=%async_computation | async-start | bytes 4194304 | tf_op jit(solution)/shard_map/all_to_all | solution.py:59
  10.2 46.7 %all-to-all-done = bf16[2,1,16,32,1024]{4,3,1,0,2:T(8,128)(2,1)S(1)} async-done(((bf16[2,1,16,32,1024]{4,3,1,0,2:T(8,128)(2,1)}), bf16[2,1,16,32,1024]{4,3,1,0,2:T(8,128)(2,1)S(1)}, u32[]{:S(2)}, u32[]{:S(2)}) %all-to-all-start) | async-done | bytes 2097184 | tf_op jit(solution)/shard_map/all_to_all | solution.py:59
  56.9 4.9 %gather_fusion.1 = bf16[48,2,32,1024]{3,2,1,0:T(8,128)(2,1)} fusion(bf16[2,16,32,1024]{3,2,0,1:T(8,128)(2,1)S(1)} %bitcast.92, s32[1024]{0:T(1024)S(1)} %pad_clamp_fusion), kind=kCustom, calls=%fused_computation.1 | custom fusion | bytes 12583104 | tf_op jit(solution)/shard_map/gather | solution.py:64
  61.8 4.8 %all-to-all-start.1 = ((bf16[2,16,3,32,1024]{4,3,0,2,1:T(8,128)(2,1)}), bf16[2,16,3,32,1024]{4,3,0,2,1:T(8,128)(2,1)}, u32[]{:S(2)}, u32[]{:S(2)}) async-start(bf16[2,16,3,32,1024]{4,3,0,2,1:T(8,128)(2,1)} %bitcast.93), calls=%async_computation.1 | async-start | bytes 12582912 | tf_op jit(solution)/shard_map/all_to_all | solution.py:65
  75.3 140.2 %collective-permute-done = bf16[2,256,1024]{1,2,0:T(8,128)(2,1)} collective-permute-done((bf16[2,256,1024]{1,2,0:T(8,128)(2,1)}, bf16[2,256,1024]{1,2,0:T(8,128)(2,1)}, u32[]{:S(2)}, u32[]{:S(2)}) %collective-permute-start) | collective-permute-done | bytes 1048608 | tf_op jit(solution)/shard_map/ppermute | solution.py:16
  225.2 12.4 %maximum_bitcast_fusion = bf16[8,2048,128]{2,0,1:T(8,128)(2,1)} fusion(bf16[512,8,128]{2,1,0:T(8,128)(2,1)S(1)} %copy-done.1, bf16[1536,8,128]{2,1,0:T(8,128)(2,1)S(1)} %bitcast.96), kind=kLoop, calls=%fused_computation.31 | loop fusion | flops 2097152 | bytes 8388608 | tf_op jit(solution)/shard_map/transpose | solution.py:29
  237.6 6.7 %copy.39 = bf16[8,2048,128]{1,2,0:T(8,128)(2,1)} copy(bf16[8,2048,128]{2,0,1:T(8,128)(2,1)} %maximum_bitcast_fusion) | data formatting | bytes 8388608 | tf_op jit(solution)/shard_map/while | solution.py:45
  245.9 11.1 %maximum_bitcast_fusion.1 = bf16[8,2048,128]{2,0,1:T(8,128)(2,1)S(1)} fusion(bf16[512,8,128]{2,1,0:T(8,128)(2,1)S(1)} %copy-done, bf16[1536,8,128]{2,1,0:T(8,128)(2,1)S(1)} %bitcast.97), kind=kLoop, calls=%fused_computation.32 | loop fusion | flops 2097152 | bytes 8388608 | tf_op jit(solution)/shard_map/transpose | solution.py:26
  259.7 93.2 %while.10 = (s32[]{:T(128)}, bf16[8,256,4,128]{1,3,2,0:T(8,128)(2,1)S(1)}, bf16[8,2048,128]{1,2,0:T(8,128)(2,1)}, pred[256,2048]{0,1:T(8,128)(4,1)S(1)}, bf16[8,...) while((s32[]{:T(128)}, bf16[8,256,4,128]{1,3,2,0:T(8,128)(2,1)S(1)}, ...), condition=%wide.region_3.4_spmd, body=%wide.region_0.3_spmd.sunk | while | flops 1086457856 | bytes 18884684 | solution.py:45
  259.7 7.3 %fusion.59 = (f32[4,256]{1,0:T(4,128)S(1)}, f32[4,256,2048]{1,2,0:T(8,128)}) fusion(pred[256,2048]{0,1:T(8,128)(4,1)S(1)} %get-tuple-element.126, bf16[8,2048,128]{2,1,0:T(8,128)(2,1)} %get-tuple-element.127, s32[]{:T(128)} %get-tuple-element.116, bf16[8,256,4,128]{1,3,2,0:T(8,128)(2,1)} %get-tuple-element.128), kind=kOutput, calls=%fused_computation.49.clone.1 | convolution fusion | flops 545261568 | bytes 9704448 | tf_op jit(solution)/shard_map/while/body/eval_jaxpr/sub | solution.py:40
  271.3 7.3 %fusion.59 = (f32[4,256]{1,0:T(4,128)S(1)}, f32[4,256,2048]{1,2,0:T(8,128)}) fusion(pred[256,2048]{0,1:T(8,128)(4,1)S(1)} %get-tuple-element.126, bf16[8,2048,128]{2,1,0:T(8,128)(2,1)} %get-tuple-element.127, s32[]{:T(128)} %get-tuple-element.116, bf16[8,256,4,128]{1,3,2,0:T(8,128)(2,1)} %get-tuple-element.128), kind=kOutput, calls=%fused_computation.49.clone.1 | convolution fusion | flops 545261568 | bytes 9704448 | tf_op jit(solution)/shard_map/while/body/eval_jaxpr/sub | solution.py:40
  278.7 4.3 %fusion.60 = bf16[8,256,4,128]{1,3,2,0:T(8,128)(2,1)S(1)} fusion(bf16[8,256,4,128]{1,3,2,0:T(8,128)(2,1)S(1)} %get-tuple-element.117, s32[]{:T(128)} %get-tuple-element.116, f32[4,256,2048]{1,2,0:T(8,128)} %get-tuple-element.107, f32[4,256]{1,0:T(4,128)S(1)} %get-tuple-element.108, bf16[8,2048,128]{1,2,0:T(8,128)(2,1)} %get-tuple-element.125), kind=kOutput, calls=%fused_computation.13.clone.1 | convolution fusion | flops 541196288 | bytes 9180160 | tf_op jit(solution)/shard_map/while/body/eval_jaxpr/grk,kd->rgd/dot_general | solution.py:42
  283.0 7.3 %fusion.59 = (f32[4,256]{1,0:T(4,128)S(1)}, f32[4,256,2048]{1,2,0:T(8,128)}) fusion(pred[256,2048]{0,1:T(8,128)(4,1)S(1)} %get-tuple-element.126, bf16[8,2048,128]{2,1,0:T(8,128)(2,1)} %get-tuple-element.127, s32[]{:T(128)} %get-tuple-element.116, bf16[8,256,4,128]{1,3,2,0:T(8,128)(2,1)} %get-tuple-element.128), kind=kOutput, calls=%fused_computation.49.clone.1 | convolution fusion | flops 545261568 | bytes 9704448 | tf_op jit(solution)/shard_map/while/body/eval_jaxpr/sub | solution.py:40
  290.3 4.3 %fusion.60 = bf16[8,256,4,128]{1,3,2,0:T(8,128)(2,1)S(1)} fusion(bf16[8,256,4,128]{1,3,2,0:T(8,128)(2,1)S(1)} %get-tuple-element.117, s32[]{:T(128)} %get-tuple-element.116, f32[4,256,2048]{1,2,0:T(8,128)} %get-tuple-element.107, f32[4,256]{1,0:T(4,128)S(1)} %get-tuple-element.108, bf16[8,2048,128]{1,2,0:T(8,128)(2,1)} %get-tuple-element.125), kind=kOutput, calls=%fused_computation.13.clone.1 | convolution fusion | flops 541196288 | bytes 9180160 | tf_op jit(solution)/shard_map/while/body/eval_jaxpr/grk,kd->rgd/dot_general | solution.py:42
  294.6 7.3 %fusion.59 = (f32[4,256]{1,0:T(4,128)S(1)}, f32[4,256,2048]{1,2,0:T(8,128)}) fusion(pred[256,2048]{0,1:T(8,128)(4,1)S(1)} %get-tuple-element.126, bf16[8,2048,128]{2,1,0:T(8,128)(2,1)} %get-tuple-element.127, s32[]{:T(128)} %get-tuple-element.116, bf16[8,256,4,128]{1,3,2,0:T(8,128)(2,1)} %get-tuple-element.128), kind=kOutput, calls=%fused_computation.49.clone.1 | convolution fusion | flops 545261568 | bytes 9704448 | tf_op jit(solution)/shard_map/while/body/eval_jaxpr/sub | solution.py:40
  302.0 4.3 %fusion.60 = bf16[8,256,4,128]{1,3,2,0:T(8,128)(2,1)S(1)} fusion(bf16[8,256,4,128]{1,3,2,0:T(8,128)(2,1)S(1)} %get-tuple-element.117, s32[]{:T(128)} %get-tuple-element.116, f32[4,256,2048]{1,2,0:T(8,128)} %get-tuple-element.107, f32[4,256]{1,0:T(4,128)S(1)} %get-tuple-element.108, bf16[8,2048,128]{1,2,0:T(8,128)(2,1)} %get-tuple-element.125), kind=kOutput, calls=%fused_computation.13.clone.1 | convolution fusion | flops 541196288 | bytes 9180160 | tf_op jit(solution)/shard_map/while/body/eval_jaxpr/grk,kd->rgd/dot_general | solution.py:42
  306.3 7.3 %fusion.59 = (f32[4,256]{1,0:T(4,128)S(1)}, f32[4,256,2048]{1,2,0:T(8,128)}) fusion(pred[256,2048]{0,1:T(8,128)(4,1)S(1)} %get-tuple-element.126, bf16[8,2048,128]{2,1,0:T(8,128)(2,1)} %get-tuple-element.127, s32[]{:T(128)} %get-tuple-element.116, bf16[8,256,4,128]{1,3,2,0:T(8,128)(2,1)} %get-tuple-element.128), kind=kOutput, calls=%fused_computation.49.clone.1 | convolution fusion | flops 545261568 | bytes 9704448 | tf_op jit(solution)/shard_map/while/body/eval_jaxpr/sub | solution.py:40
  313.6 4.3 %fusion.60 = bf16[8,256,4,128]{1,3,2,0:T(8,128)(2,1)S(1)} fusion(bf16[8,256,4,128]{1,3,2,0:T(8,128)(2,1)S(1)} %get-tuple-element.117, s32[]{:T(128)} %get-tuple-element.116, f32[4,256,2048]{1,2,0:T(8,128)} %get-tuple-element.107, f32[4,256]{1,0:T(4,128)S(1)} %get-tuple-element.108, bf16[8,2048,128]{1,2,0:T(8,128)(2,1)} %get-tuple-element.125), kind=kOutput, calls=%fused_computation.13.clone.1 | convolution fusion | flops 541196288 | bytes 9180160 | tf_op jit(solution)/shard_map/while/body/eval_jaxpr/grk,kd->rgd/dot_general | solution.py:42
  317.9 7.3 %fusion.59 = (f32[4,256]{1,0:T(4,128)S(1)}, f32[4,256,2048]{1,2,0:T(8,128)}) fusion(pred[256,2048]{0,1:T(8,128)(4,1)S(1)} %get-tuple-element.126, bf16[8,2048,128]{2,1,0:T(8,128)(2,1)} %get-tuple-element.127, s32[]{:T(128)} %get-tuple-element.116, bf16[8,256,4,128]{1,3,2,0:T(8,128)(2,1)} %get-tuple-element.128), kind=kOutput, calls=%fused_computation.49.clone.1 | convolution fusion | flops 545261568 | bytes 9704448 | tf_op jit(solution)/shard_map/while/body/eval_jaxpr/sub | solution.py:40
  325.3 4.3 %fusion.60 = bf16[8,256,4,128]{1,3,2,0:T(8,128)(2,1)S(1)} fusion(bf16[8,256,4,128]{1,3,2,0:T(8,128)(2,1)S(1)} %get-tuple-element.117, s32[]{:T(128)} %get-tuple-element.116, f32[4,256,2048]{1,2,0:T(8,128)} %get-tuple-element.107, f32[4,256]{1,0:T(4,128)S(1)} %get-tuple-element.108, bf16[8,2048,128]{1,2,0:T(8,128)(2,1)} %get-tuple-element.125), kind=kOutput, calls=%fused_computation.13.clone.1 | convolution fusion | flops 541196288 | bytes 9180160 | tf_op jit(solution)/shard_map/while/body/eval_jaxpr/grk,kd->rgd/dot_general | solution.py:42
  329.6 7.3 %fusion.59 = (f32[4,256]{1,0:T(4,128)S(1)}, f32[4,256,2048]{1,2,0:T(8,128)}) fusion(pred[256,2048]{0,1:T(8,128)(4,1)S(1)} %get-tuple-element.126, bf16[8,2048,128]{2,1,0:T(8,128)(2,1)} %get-tuple-element.127, s32[]{:T(128)} %get-tuple-element.116, bf16[8,256,4,128]{1,3,2,0:T(8,128)(2,1)} %get-tuple-element.128), kind=kOutput, calls=%fused_computation.49.clone.1 | convolution fusion | flops 545261568 | bytes 9704448 | tf_op jit(solution)/shard_map/while/body/eval_jaxpr/sub | solution.py:40
  336.9 4.3 %fusion.60 = bf16[8,256,4,128]{1,3,2,0:T(8,128)(2,1)S(1)} fusion(bf16[8,256,4,128]{1,3,2,0:T(8,128)(2,1)S(1)} %get-tuple-element.117, s32[]{:T(128)} %get-tuple-element.116, f32[4,256,2048]{1,2,0:T(8,128)} %get-tuple-element.107, f32[4,256]{1,0:T(4,128)S(1)} %get-tuple-element.108, bf16[8,2048,128]{1,2,0:T(8,128)(2,1)} %get-tuple-element.125), kind=kOutput, calls=%fused_computation.13.clone.1 | convolution fusion | flops 541196288 | bytes 9180160 | tf_op jit(solution)/shard_map/while/body/eval_jaxpr/grk,kd->rgd/dot_general | solution.py:42
  341.3 7.3 %fusion.59 = (f32[4,256]{1,0:T(4,128)S(1)}, f32[4,256,2048]{1,2,0:T(8,128)}) fusion(pred[256,2048]{0,1:T(8,128)(4,1)S(1)} %get-tuple-element.126, bf16[8,2048,128]{2,1,0:T(8,128)(2,1)} %get-tuple-element.127, s32[]{:T(128)} %get-tuple-element.116, bf16[8,256,4,128]{1,3,2,0:T(8,128)(2,1)} %get-tuple-element.128), kind=kOutput, calls=%fused_computation.49.clone.1 | convolution fusion | flops 545261568 | bytes 9704448 | tf_op jit(solution)/shard_map/while/body/eval_jaxpr/sub | solution.py:40
  348.6 4.3 %fusion.60 = bf16[8,256,4,128]{1,3,2,0:T(8,128)(2,1)S(1)} fusion(bf16[8,256,4,128]{1,3,2,0:T(8,128)(2,1)S(1)} %get-tuple-element.117, s32[]{:T(128)} %get-tuple-element.116, f32[4,256,2048]{1,2,0:T(8,128)} %get-tuple-element.107, f32[4,256]{1,0:T(4,128)S(1)} %get-tuple-element.108, bf16[8,2048,128]{1,2,0:T(8,128)(2,1)} %get-tuple-element.125), kind=kOutput, calls=%fused_computation.13.clone.1 | convolution fusion | flops 541196288 | bytes 9180160 | tf_op jit(solution)/shard_map/while/body/eval_jaxpr/grk,kd->rgd/dot_general | solution.py:42
  (48 shorter events, 33.7 us)
Async XLA Ops:
  0.0 9.2 %copy-start.6 = (s32[8,3]{0,1:T(4,128)S(1)}, s32[8,3]{0,1:T(4,128)}, u32[]{:S(2)}) copy-start(s32[8,3]{0,1:T(4,128)} %param.13) | copy-start | bytes 292
  3.1 53.8 %all-to-all-start = ((bf16[2,1,16,32,1024]{4,3,1,0,2:T(8,128)(2,1)}), bf16[2,1,16,32,1024]{4,3,1,0,2:T(8,128)(2,1)S(1)}, u32[]{:S(2)}, u32[]{:S(2)}) async-start(bf16[2,1,16,32,1024]{4,3,1,0,2:T(8,128)(2,1)} %pad_maximum_fusion), calls=%async_computation | async-start | bytes 4194304 | tf_op jit(solution)/shard_map/all_to_all | solution.py:59
  61.8 4.8 %copy-start.4 = (bf16[256,1024]{1,0:T(8,128)(2,1)S(1)}, bf16[256,1024]{1,0:T(8,128)(2,1)}, u32[]{:S(2)}) copy-start(bf16[256,1024]{1,0:T(8,128)(2,1)} %param.9) | copy-start | bytes 1572868
  61.8 158.2 %all-to-all-start.1 = ((bf16[2,16,3,32,1024]{4,3,0,2,1:T(8,128)(2,1)}), bf16[2,16,3,32,1024]{4,3,0,2,1:T(8,128)(2,1)}, u32[]{:S(2)}, u32[]{:S(2)}) async-start(bf16[2,16,3,32,1024]{4,3,0,2,1:T(8,128)(2,1)} %bitcast.93), calls=%async_computation.1 | async-start | bytes 12582912 | tf_op jit(solution)/shard_map/all_to_all | solution.py:65
  66.6 5.0 %copy-start.2 = (bf16[256,4096]{1,0:T(8,128)(2,1)S(1)}, bf16[256,4096]{1,0:T(8,128)(2,1)}, u32[]{:S(2)}) copy-start(bf16[256,4096]{1,0:T(8,128)(2,1)} %param.8) | copy-start | bytes 6291460
  69.4 146.1 %collective-permute-start = (bf16[2,256,1024]{1,2,0:T(8,128)(2,1)}, bf16[2,256,1024]{1,2,0:T(8,128)(2,1)}, u32[]{:S(2)}, u32[]{:S(2)}) collective-permute-start(bf16[2,256,1024]{1,2,0:T(8,128)(2,1)} %pad_maximum_fusion.1), channel_id=1, source_target_pairs={{0,1},{1,2},{2,3},{3,4},{4,5},{5,6},{6,7},{7,8},{8,9},{9,10},{10,1... | collective-permute-start | bytes 3145736 | tf_op jit(solution)/shard_map/ppermute | solution.py:16
  224.0 1.2 copy-start.1
  244.6 1.2 copy-start
  256.9 2.7 copy-start.3
  257.0 2.7 copy-start.5
where the time goes:
time: 357 us; the launch traced here: 356 us
  waiting for transfers between devices  187 us (52%)
  matrix products  93 us (26%)
  local copies, waits for them, and re-layouts  32.9 us (9%)
  other arithmetic  29.3 us (8%)
  starting transfers between devices  13.2 us (4%)
    ppermute x1, waiting for transfers between devices, passed_along(): return lax.ppermute(block, axis, route)  140 us
    sub x8, matrix products, one_head(): expon = jnp.exp(scores - largest)  58.7 us
    all_to_all x1, waiting for transfers between devices, per_device(): lax.all_to_all(stacked, 'seq', split_axis=2, concat_axis=1, tiled=True)  46.7 us
    dot_general x8, matrix products, one_head(): jnp.einsum('grk,kd->rgd', weights, head_values, preferred_element_type=jn...  34.3 us
    transpose x1, other arithmetic, attend_local(): jnp.moveaxis(rows_of_values.reshape(count_of_keys, KEY_VALUE_HEADS, HEAD_...  12.4 us
    transpose x1, other arithmetic, attend_local(): jnp.moveaxis(rows_of_keys.reshape(count_of_keys, KEY_VALUE_HEADS, HEAD_SI...  11.1 us
    while x2, local copies, waits for them, and re-layouts, attend_local(): lax.map(one_head, (heads_of_queries, heads_of_keys, heads_of_values))  9.38 us
  transfers between devices with their start and end apart: 3, of which 2 were waited for; matrix products, arithmetic and copies ran while one was open for 3% of the time, Pallas kernels for 0%

commit v1 on v0

v1 whole, which is shorter than its diff:
```python
import functools

import jax
import jax.numpy as jnp
from jax import lax
from jax.experimental import pallas as pl
from jax.experimental.pallas import tpu as pltpu
from jax.sharding import PartitionSpec as P

QUERY_HEADS = 32
KEY_VALUE_HEADS = 8
HEAD_SIZE = 128
BLK = 512
TOPK = 3
CORES = 2
CHUNKS = KEY_VALUE_HEADS // CORES
SHARE = QUERY_HEADS // KEY_VALUE_HEADS
WIDE = SHARE * HEAD_SIZE
SCALE = HEAD_SIZE ** (-0.5) * 1.4426950408889634
MESH = pl.DeviceIdType.MESH


def attend_rows(q, keys, values, own_keys, own_values, first_row):
    contract = (((1,), (1,)), ((), ()))
    scores = lax.dot_general(q, keys, contract, preferred_element_type=jnp.float32)
    own = lax.dot_general(q, own_keys, contract, preferred_element_type=jnp.float32)
    row = lax.broadcasted_iota(jnp.int32, own.shape, 0) + first_row
    column = lax.broadcasted_iota(jnp.int32, own.shape, 1)
    own = jnp.where(column <= row, own, -1e30)
    largest = jnp.maximum(
        jnp.max(scores, axis=-1, keepdims=True), jnp.max(own, axis=-1, keepdims=True)
    ) * SCALE
    weights = jnp.exp2(scores * SCALE - largest).astype(jnp.bfloat16)
    own_weights = jnp.exp2(own * SCALE - largest).astype(jnp.bfloat16)

    def with_ones(block):
        return jnp.concatenate([block, jnp.ones_like(block)], axis=1)

    both = jnp.dot(weights, with_ones(values), preferred_element_type=jnp.float32)
    both += jnp.dot(own_weights, with_ones(own_values), preferred_element_type=jnp.float32)
    return (both[:, :HEAD_SIZE] / both[:, HEAD_SIZE:]).astype(jnp.bfloat16)


def kernel(
    members, holders,
    selected, queries, stretch_keys, stretch_values, cache_keys, cache_values,
    out,
    *scratch,
):
    held = scratch[:CHUNKS]
    staged, packed, kv, qs, outs = scratch[CHUNKS:CHUNKS + 5]
    (stage_sem, spread_send, spread_recv, fetch_send, fetch_recv,
     own_send, own_recv, q_send, q_recv, o_send, o_recv, o_local) = scratch[CHUNKS + 5:]

    me = lax.axis_index("seq")
    core = lax.rem(me, CORES)
    sibling = me + 1 - 2 * core
    base = (me // holders) * holders
    mine = lax.rem(me, holders)
    half = queries.shape[0]
    piece = BLK // holders
    my_rows = pl.ds(pl.multiple_of(core * half, half), half)
    other_rows = pl.ds(pl.multiple_of((1 - core) * half, half), half)

    for h in range(CHUNKS):
        for c in range(CORES):
            lanes = pl.ds((c * CHUNKS + h) * HEAD_SIZE, HEAD_SIZE)
            for n, source in enumerate((cache_keys, cache_values)):
                pltpu.make_async_copy(
                    source.at[:, lanes], staged.at[h, c, n], stage_sem.at[h]
                ).start()

    barrier = pltpu.get_barrier_semaphore()

    @pl.loop(1, members)
    def _(k):
        pl.semaphore_signal(
            barrier, inc=1, device_id={"seq": lax.rem(me + k, members)}, device_id_type=MESH
        )

    pl.semaphore_wait(barrier, members - 1)

    def spread(h):
        pltpu.make_async_copy(staged.at[h], staged.at[h], stage_sem.at[h]).wait()
        pltpu.make_async_copy(
            staged.at[h, :, :, pl.ds(pl.multiple_of(mine * piece, piece), piece), :],
            held[h].at[me], spread_recv.at[h],
        ).start()

        @pl.loop(1, members)
        def _(k):
            to = lax.rem(me + k, members)
            part = pl.multiple_of(lax.rem(to, holders) * piece, piece)
            pltpu.make_async_remote_copy(
                src_ref=staged.at[h, :, :, pl.ds(part, piece), :],
                dst_ref=held[h].at[me],
                send_sem=spread_send.at[h],
                recv_sem=spread_recv.at[h],
                device_id={"seq": to},
                device_id_type=MESH,
            ).start()

    spread(0)

    for h in range(CHUNKS):
        for here in (True, False):
            c = core if here else 1 - core
            q_lanes = pl.ds(pl.multiple_of((c * CHUNKS + h) * WIDE, WIDE), WIDE)
            kv_lanes = pl.ds(pl.multiple_of((c * CHUNKS + h) * HEAD_SIZE, HEAD_SIZE), HEAD_SIZE)
            for source, target, send, recv in (
                (queries.at[:, q_lanes], qs.at[h, my_rows, :], q_send, q_recv),
                (stretch_keys.at[:, kv_lanes], kv.at[h, TOPK, 0, my_rows, :], own_send, own_recv),
                (stretch_values.at[:, kv_lanes], kv.at[h, TOPK, 1, my_rows, :], own_send, own_recv),
            ):
                if here:
                    pltpu.make_async_copy(source, target, recv.at[h]).start()
                else:
                    pltpu.make_async_remote_copy(
                        src_ref=source, dst_ref=target, send_sem=send, recv_sem=recv.at[h],
                        device_id={"seq": sibling}, device_id_type=MESH,
                    ).start()

    for h in range(1, CHUNKS):
        spread(h)

    def fetch(h):
        pltpu.make_async_copy(held[h], held[h], spread_recv.at[h]).wait()
        land = kv.at[h, pl.ds(0, TOPK), :, pl.ds(pl.multiple_of(mine * piece, piece), piece), :]

        @pl.loop(0, holders)
        def _(k):
            i = lax.rem(mine + k, holders)
            to = base + i
            for t in range(TOPK):
                block = selected[to // CORES, t]
                packed[h, i, t] = held[h][block, lax.rem(to, CORES)]

            @pl.when(k == 0)
            def _():
                pltpu.make_async_copy(packed.at[h, i], land, fetch_recv.at[h]).start()

            @pl.when(k > 0)
            def _():
                pltpu.make_async_remote_copy(
                    src_ref=packed.at[h, i], dst_ref=land,
                    send_sem=fetch_send.at[h], recv_sem=fetch_recv.at[h],
                    device_id={"seq": to}, device_id_type=MESH,
                ).start()

    def attend(h):
        chosen = kv.at[h, pl.ds(0, TOPK)]
        pltpu.make_async_copy(chosen, chosen, fetch_recv.at[h]).wait()
        pltpu.make_async_copy(kv.at[h, TOPK], kv.at[h, TOPK], own_recv.at[h]).wait()
        pltpu.make_async_copy(qs.at[h], qs.at[h], q_recv.at[h]).wait()

        @pl.loop(0, SHARE)
        def _(g):
            lanes = pl.ds(pl.multiple_of(g * HEAD_SIZE, HEAD_SIZE), HEAD_SIZE)
            for r in range(CORES):
                rows = pl.ds(r * half, half)
                keys = kv[h, 0:TOPK, 0].reshape(TOPK * BLK, HEAD_SIZE)
                values = kv[h, 0:TOPK, 1].reshape(TOPK * BLK, HEAD_SIZE)
                seen = (r + 1) * half
                outs[h, rows, lanes] = attend_rows(
                    qs[h, rows, lanes], keys, values,
                    kv[h, TOPK, 0, 0:seen], kv[h, TOPK, 1, 0:seen], r * half,
                )

        lanes = pl.ds(pl.multiple_of((core * CHUNKS + h) * WIDE, WIDE), WIDE)
        pltpu.make_async_copy(outs.at[h, my_rows, :], out.at[:, lanes], o_local).start()
        pltpu.make_async_remote_copy(
            src_ref=outs.at[h, other_rows, :], dst_ref=out.at[:, lanes],
            send_sem=o_send, recv_sem=o_recv,
            device_id={"seq": sibling}, device_id_type=MESH,
        ).start()

    @pl.loop(0, CHUNKS + 1)
    def _(step):
        for h in range(CHUNKS):
            pl.when(step == h)(functools.partial(fetch, h))

        @pl.when(step > 0)
        def _():
            attend(step - 1)

    for h in range(CHUNKS):
        sent = held[h].at[pl.ds(0, members - 1)]
        pltpu.make_async_copy(sent, sent, spread_send.at[h]).wait()
        sent = packed.at[h, pl.ds(0, holders - 1)]
        pltpu.make_async_copy(sent, sent, fetch_send.at[h]).wait()
    sent = qs.at[pl.ds(0, CHUNKS // 2)]
    pltpu.make_async_copy(sent, sent, q_send).wait()
    sent = kv.at[pl.ds(0, CHUNKS // 2), TOPK]
    pltpu.make_async_copy(sent, sent, own_send).wait()
    wide = CHUNKS * WIDE
    kept = out.at[:, pl.ds(pl.multiple_of(core * wide, wide), wide)]
    given = out.at[:, pl.ds(pl.multiple_of((1 - core) * wide, wide), wide)]
    pltpu.make_async_copy(kept, kept, o_local).wait()
    pltpu.make_async_copy(kept, kept, o_send).wait()
    pltpu.make_async_copy(given, given, o_recv).wait()


def per_device(queries, stretch_keys, stretch_values, cache_keys, cache_values, selected):
    members = lax.axis_size("seq")
    half = queries.shape[0]
    assert half * CORES == BLK and cache_keys.shape[0] == BLK
    holders = min(members // 2, BLK // 16)
    piece = BLK // holders
    bf16 = jnp.bfloat16
    dma = pltpu.SemaphoreType.DMA
    anywhere = pl.BlockSpec(memory_space=pl.ANY)
    return pl.pallas_call(
        functools.partial(kernel, members, holders),
        out_shape=jax.ShapeDtypeStruct(queries.shape, bf16),
        in_specs=[pl.BlockSpec(memory_space=pltpu.SMEM)] + [anywhere] * 5,
        out_specs=anywhere,
        scratch_shapes=[
            pltpu.VMEM((members, CORES, 2, piece, HEAD_SIZE), bf16) for _ in range(CHUNKS)
        ] + [
            pltpu.VMEM((CHUNKS, CORES, 2, BLK, HEAD_SIZE), bf16),
            pltpu.VMEM((CHUNKS, holders, TOPK, 2, piece, HEAD_SIZE), bf16),
            pltpu.VMEM((CHUNKS, TOPK + 1, 2, BLK, HEAD_SIZE), bf16),
            pltpu.VMEM((CHUNKS, BLK, WIDE), bf16),
            pltpu.VMEM((CHUNKS, BLK, WIDE), bf16),
            dma((CHUNKS,)), dma((CHUNKS,)), dma((CHUNKS,)), dma((CHUNKS,)), dma((CHUNKS,)),
            dma, dma((CHUNKS,)), dma, dma((CHUNKS,)), dma, dma, dma,
        ],
        compiler_params=pltpu.CompilerParams(
            collective_id=0, has_side_effects=True, vmem_limit_bytes=56 * 1024 * 1024
        ),
        cost_estimate=pl.CostEstimate(
            flops=4 * half * QUERY_HEADS * HEAD_SIZE * (TOPK + 1) * BLK,
            bytes_accessed=16 << 20,
            transcendentals=half * QUERY_HEADS * (TOPK + 1) * BLK,
        ),
    )(selected, queries, stretch_keys, stretch_values, cache_keys, cache_values)


def solution(mesh):
    split = P(("groups", "seq"), None)
    return jax.shard_map(
        per_device,
        mesh=mesh,
        in_specs=(split, split, split, split, split, P("groups", None)),
        out_specs=split,
        check_vma=False,
    )
```

time: 357 us -> 128 us (0.36)
  the two profiles are of different devices: /device:TPU:16 before, /device:TPU:0 now
where the time goes in v1:
time: 128 us; the launch traced here: 127 us
  Pallas kernels  122 us (95%)
  local copies, waits for them, and re-layouts  4.48 us (4%)
    pallas_call x1, Pallas kernels, per_device(): pl.pallas_call(functools.partial(kernel, members, holders), out_shape=jax...  122 us
    unnamed x2, local copies, waits for them, and re-layouts  4.48 us

profile of v1, /device:TPU:0, one launch (start us, length us, event | category | flops | bytes accessed | tf_op | source)
XLA Modules:
  0.0 126.6 jit_solution(3290598295194119284)
XLA Ops:
  0.0 1.3 %copy.7.selected = s32[8,3]{1,0:T(8,128)} copy(s32[8,3]{0,1:T(4,128)} %param.11) | data formatting | bytes 192 | tf_op args[5]
  1.3 122.1 %shard_map.64 = bf16[256,4096]{1,0:T(8,128)(2,1)} custom-call(s32[8,3]{1,0:T(8,128)} %copy.7.selected, bf16[256,4096]{1,0:T(8,128)(2,1)} %queries.1, bf16[256,1024]{1,0:T(8,128)(2,1)} %stretch_keys.1, bf16[256,1024]{1,0:T(8,128)(2,1)} %stretch_values.1, bf16[512,1024]{1,0:T(8,128)(2,1)} %cache_keys.1, bf16[512,1024]{1,0:T(8,128)(2,1)} %cache_values.1), custom_call_target="tpu_custom_call" | custom-call | flops 8589934592 | bytes 16777216 | tf_op jit(solution)/shard_map/pallas_call | solution.py:212
  123.4 3.1 %copy.9 = bf16[256,4096]{1,0:T(8,128)(2,1)} copy(bf16[256,4096]{1,0:T(8,128)(2,1)} %shard_map.64) | data formatting | bytes 4194304

commit v2 on v1

v2 whole, which is shorter than its diff:
```python
import functools

import jax
import jax.numpy as jnp
from jax import lax
from jax.experimental import pallas as pl
from jax.experimental.pallas import tpu as pltpu
from jax.sharding import PartitionSpec as P

QUERY_HEADS = 32
KEY_VALUE_HEADS = 8
HEAD_SIZE = 128
BLK = 512
TOPK = 3
CORES = 2
CHUNKS = KEY_VALUE_HEADS // CORES
STAGES = 2 * CHUNKS
SHARE = QUERY_HEADS // KEY_VALUE_HEADS
WIDE = SHARE * HEAD_SIZE
SCALE = HEAD_SIZE ** (-0.5) * 1.4426950408889634
MESH = pl.DeviceIdType.MESH


CONTRACT = (((1,), (1,)), ((), ()))


def weighted(scores, largest, values):
    weights = jnp.exp2(scores * SCALE - largest * SCALE).astype(jnp.bfloat16)
    both = jnp.concatenate([values, jnp.ones_like(values)], axis=1)
    return jnp.dot(weights, both, preferred_element_type=jnp.float32)


def product(q, keys):
    return lax.dot_general(q, keys, CONTRACT, preferred_element_type=jnp.float32)


def attend_first(q, keys, values, own_keys, own_values, first_row):
    scores, own = product(q, keys), product(q, own_keys)
    row = lax.broadcasted_iota(jnp.int32, own.shape, 0) + first_row
    column = lax.broadcasted_iota(jnp.int32, own.shape, 1)
    own = jnp.where(column <= row, own, -1e30)
    largest = jnp.maximum(
        jnp.max(scores, axis=-1, keepdims=True), jnp.max(own, axis=-1, keepdims=True)
    )
    return weighted(scores, largest, values) + weighted(own, largest, own_values), largest


def attend_last(q, keys, values, both, before):
    scores = product(q, keys)
    largest = jnp.maximum(before, jnp.max(scores, axis=-1, keepdims=True))
    both = both * jnp.exp2((before - largest) * SCALE) + weighted(scores, largest, values)
    return (both[:, :HEAD_SIZE] / both[:, HEAD_SIZE:]).astype(jnp.bfloat16)


def kernel(
    members, holders, relayed,
    selected, queries, stretch_keys, stretch_values, cache_keys, cache_values,
    out,
    *scratch,
):
    held = scratch[:STAGES]
    staged, packed, kv, own, qs, outs, sums, tops = scratch[STAGES:STAGES + 8]
    (stage_sem, spread_send, spread_recv, near_recv, relay_send, fetch_send, fetch_recv,
     own_send, own_recv, q_send, q_recv, o_send, o_recv, o_local) = scratch[STAGES + 8:]

    me = lax.axis_index("seq")
    core = lax.rem(me, CORES)
    sibling = me + 1 - 2 * core
    mine = lax.rem(me, holders)
    if relayed:
        plane = me // holders
        upper = plane // 2
        set_size = 2 * holders
        base = upper * set_size
        inner = (1 + upper) * holders
        outer = 3 * upper * holders
        facing = (2 - upper) * holders
        away = lax.rem(plane + upper + 1, 2)
    else:
        set_size = holders
        base = (me // holders) * holders
    half = queries.shape[0]
    piece = BLK // (2 * holders)
    my_rows = pl.ds(pl.multiple_of(core * half, half), half)
    other_rows = pl.ds(pl.multiple_of((1 - core) * half, half), half)

    for h in range(CHUNKS):
        for c in range(CORES):
            lanes = pl.ds((c * CHUNKS + h) * HEAD_SIZE, HEAD_SIZE)
            for n, source in enumerate((cache_keys, cache_values)):
                pltpu.make_async_copy(
                    source.at[:, lanes], staged.at[h, c, n], stage_sem.at[h]
                ).start()

    barrier = pltpu.get_barrier_semaphore()

    @pl.loop(1, members)
    def _(k):
        pl.semaphore_signal(
            barrier, inc=1, device_id={"seq": lax.rem(me + k, members)}, device_id_type=MESH
        )

    pl.semaphore_wait(barrier, members - 1)

    def rows_of(s, holder):
        first = (s % 2) * (BLK // 2) + holder * piece
        return pl.ds(pl.multiple_of(first, piece), piece)

    def spread_near(s):
        h = s // 2

        @pl.loop(0, holders)
        def _(k):
            q = lax.rem(mine + k, holders)
            source = staged.at[h, :, :, rows_of(s, q), :]

            @pl.when(inner + q == me)
            def _():
                pltpu.make_async_copy(source, held[s].at[me], near_recv.at[s, away]).start()

            @pl.when(inner + q != me)
            def _():
                pltpu.make_async_remote_copy(
                    src_ref=source, dst_ref=held[s].at[me],
                    send_sem=spread_send.at[s], recv_sem=near_recv.at[s, away],
                    device_id={"seq": inner + q}, device_id_type=MESH,
                ).start()

    def relay(s):
        for n, first in enumerate((inner, outer)):
            blocks = held[s].at[pl.ds(first, holders)]
            pltpu.make_async_copy(blocks, blocks, near_recv.at[s, n]).wait()
            pltpu.make_async_remote_copy(
                src_ref=blocks, dst_ref=blocks,
                send_sem=relay_send.at[s], recv_sem=spread_recv.at[s],
                device_id={"seq": facing + mine}, device_id_type=MESH,
            ).start()

    def spread(s):
        h = s // 2
        if s % 2 == 0:
            pltpu.make_async_copy(staged.at[h], staged.at[h], stage_sem.at[h]).wait()
        if relayed:
            spread_near(s)
            return
        pltpu.make_async_copy(
            staged.at[h, :, :, rows_of(s, mine), :], held[s].at[me], spread_recv.at[s]
        ).start()

        @pl.loop(1, members)
        def _(k):
            to = lax.rem(me + k, members)
            pltpu.make_async_remote_copy(
                src_ref=staged.at[h, :, :, rows_of(s, lax.rem(to, holders)), :],
                dst_ref=held[s].at[me],
                send_sem=spread_send.at[s],
                recv_sem=spread_recv.at[s],
                device_id={"seq": to},
                device_id_type=MESH,
            ).start()

    spread(0)

    def holding(body, s):
        if relayed:
            pl.when(away == 0)(functools.partial(body, s))
        else:
            body(s)


    if relayed:
        spread(1)
        for s in range(2):
            holding(relay, s)
    for h in range(CHUNKS):
        for here in (True, False):
            c = core if here else 1 - core
            q_lanes = pl.ds(pl.multiple_of((c * CHUNKS + h) * WIDE, WIDE), WIDE)
            kv_lanes = pl.ds(pl.multiple_of((c * CHUNKS + h) * HEAD_SIZE, HEAD_SIZE), HEAD_SIZE)
            for source, target, send, recv in (
                (queries.at[:, q_lanes], qs.at[h, my_rows, :], q_send, q_recv),
                (stretch_keys.at[:, kv_lanes], own.at[h, 0, my_rows, :], own_send, own_recv),
                (stretch_values.at[:, kv_lanes], own.at[h, 1, my_rows, :], own_send, own_recv),
            ):
                if here:
                    pltpu.make_async_copy(source, target, recv.at[h]).start()
                else:
                    pltpu.make_async_remote_copy(
                        src_ref=source, dst_ref=target, send_sem=send, recv_sem=recv.at[h],
                        device_id={"seq": sibling}, device_id_type=MESH,
                    ).start()

    for s in range(2 if relayed else 1, STAGES if not relayed else 3):
        spread(s)

    def fetch(s):
        arrived = held[s].at[pl.ds(0, set_size)] if relayed else held[s]
        pltpu.make_async_copy(arrived, arrived, spread_recv.at[s]).wait()
        land = kv.at[s, :, :, pl.ds(pl.multiple_of(mine * piece, piece), piece), :]

        here = me - base

        @pl.loop(0, set_size)
        def _(k):
            i = lax.rem(here + k, set_size)
            to = base + i
            for t in range(TOPK):
                block = selected[t, to // CORES]
                packed[s, i, t] = held[s][block, lax.rem(to, CORES)]

            @pl.when(k == 0)
            def _():
                pltpu.make_async_copy(packed.at[s, i], land, fetch_recv.at[s]).start()

            @pl.when(k > 0)
            def _():
                pltpu.make_async_remote_copy(
                    src_ref=packed.at[s, i], dst_ref=land,
                    send_sem=fetch_send.at[s], recv_sem=fetch_recv.at[s],
                    device_id={"seq": to}, device_id_type=MESH,
                ).start()

    def picked(s, n):
        return kv[s, :, n].reshape(TOPK * BLK // 2, HEAD_SIZE)

    def tiles(body):
        @pl.loop(0, SHARE // 2)
        def _(pair):
            for u in range(2):
                g = pair * 2 + u
                lanes = pl.ds(pl.multiple_of(g * HEAD_SIZE, HEAD_SIZE), HEAD_SIZE)
                for r in range(CORES):
                    body(g, lanes, r, pl.ds(r * half, half))

    def first_part(h):
        s = 2 * h
        pltpu.make_async_copy(kv.at[s], kv.at[s], fetch_recv.at[s]).wait()
        pltpu.make_async_copy(own.at[h], own.at[h], own_recv.at[h]).wait()
        pltpu.make_async_copy(qs.at[h], qs.at[h], q_recv.at[h]).wait()

        def body(g, lanes, r, rows):
            seen = (r + 1) * half
            both, largest = attend_first(
                qs[h, rows, lanes], picked(s, 0), picked(s, 1),
                own[h, 0, 0:seen], own[h, 1, 0:seen], r * half,
            )
            sums[g, rows] = both
            tops[g, rows] = jnp.broadcast_to(largest, (half, HEAD_SIZE))

        tiles(body)

    def last_part(h):
        s = 2 * h + 1
        pltpu.make_async_copy(kv.at[s], kv.at[s], fetch_recv.at[s]).wait()

        def body(g, lanes, r, rows):
            outs[h, rows, lanes] = attend_last(
                qs[h, rows, lanes], picked(s, 0), picked(s, 1),
                sums[g, rows], tops[g, rows][:, :1],
            )

        tiles(body)

        lanes = pl.ds(pl.multiple_of((core * CHUNKS + h) * WIDE, WIDE), WIDE)
        pltpu.make_async_copy(outs.at[h, my_rows, :], out.at[:, lanes], o_local).start()
        pltpu.make_async_remote_copy(
            src_ref=outs.at[h, other_rows, :], dst_ref=out.at[:, lanes],
            send_sem=o_send, recv_sem=o_recv,
            device_id={"seq": sibling}, device_id_type=MESH,
        ).start()

    @pl.loop(0, STAGES + 1)
    def _(step):
        for s in range(STAGES):
            @pl.when(step == s)
            def _():
                if relayed and s + 2 < STAGES:
                    holding(relay, s + 2)
                if relayed and s + 3 < STAGES:
                    spread(s + 3)
                holding(fetch, s)

        @pl.when((step > 0) & (lax.rem(step, 2) == 1))
        def _():
            first_part((step - 1) // 2)

        @pl.when((step > 0) & (lax.rem(step, 2) == 0))
        def _():
            last_part((step - 1) // 2)

    def await_sent(count, s):
        sent = held[s].at[pl.ds(0, count)]
        pltpu.make_async_copy(sent, sent, spread_send.at[s]).wait()

    def await_held_sent(s):
        if relayed:
            await_sent(holders - 1, s)
            sent = held[s].at[pl.ds(0, set_size)]
            pltpu.make_async_copy(sent, sent, relay_send.at[s]).wait()
        sent = packed.at[s, pl.ds(0, set_size - 1)]
        pltpu.make_async_copy(sent, sent, fetch_send.at[s]).wait()

    for s in range(STAGES):
        if relayed:
            pl.when(away == 1)(functools.partial(await_sent, holders, s))
        else:
            await_sent(members - 1, s)
        holding(await_held_sent, s)
    sent = qs.at[pl.ds(0, CHUNKS // 2)]
    pltpu.make_async_copy(sent, sent, q_send).wait()
    sent = own.at[pl.ds(0, CHUNKS // 2)]
    pltpu.make_async_copy(sent, sent, own_send).wait()
    wide = CHUNKS * WIDE
    kept = out.at[:, pl.ds(pl.multiple_of(core * wide, wide), wide)]
    given = out.at[:, pl.ds(pl.multiple_of((1 - core) * wide, wide), wide)]
    pltpu.make_async_copy(kept, kept, o_local).wait()
    pltpu.make_async_copy(kept, kept, o_send).wait()
    pltpu.make_async_copy(given, given, o_recv).wait()


def per_device(queries, stretch_keys, stretch_values, cache_keys, cache_values, selected):
    members = lax.axis_size("seq")
    half = queries.shape[0]
    assert half * CORES == BLK and cache_keys.shape[0] == BLK
    relayed = members == 16
    holders = members // 4 if relayed else min(members // 2, BLK // 32)
    set_size = 2 * holders if relayed else holders
    piece = BLK // (2 * holders)
    bf16 = jnp.bfloat16
    dma = pltpu.SemaphoreType.DMA
    anywhere = pl.BlockSpec(memory_space=pl.ANY)
    return pl.pallas_call(
        functools.partial(kernel, members, holders, relayed),
        out_shape=jax.ShapeDtypeStruct(queries.shape, bf16),
        in_specs=[pl.BlockSpec(memory_space=pltpu.SMEM)] + [anywhere] * 5,
        out_specs=anywhere,
        scratch_shapes=[
            pltpu.VMEM((members, CORES, 2, piece, HEAD_SIZE), bf16) for _ in range(STAGES)
        ] + [
            pltpu.VMEM((CHUNKS, CORES, 2, BLK, HEAD_SIZE), bf16),
            pltpu.VMEM((STAGES, set_size, TOPK, 2, piece, HEAD_SIZE), bf16),
            pltpu.VMEM((STAGES, TOPK, 2, BLK // 2, HEAD_SIZE), bf16),
            pltpu.VMEM((CHUNKS, 2, BLK, HEAD_SIZE), bf16),
            pltpu.VMEM((CHUNKS, BLK, WIDE), bf16),
            pltpu.VMEM((CHUNKS, BLK, WIDE), bf16),
            pltpu.VMEM((SHARE, BLK, 2 * HEAD_SIZE), jnp.float32),
            pltpu.VMEM((SHARE, BLK, HEAD_SIZE), jnp.float32),
            dma((CHUNKS,)), dma((STAGES,)), dma((STAGES,)), dma((STAGES, 2)), dma((STAGES,)),
            dma((STAGES,)), dma((STAGES,)),
            dma, dma((CHUNKS,)), dma, dma((CHUNKS,)), dma, dma, dma,
        ],
        compiler_params=pltpu.CompilerParams(
            collective_id=0, has_side_effects=True, vmem_limit_bytes=56 * 1024 * 1024
        ),
        cost_estimate=pl.CostEstimate(
            flops=4 * half * QUERY_HEADS * HEAD_SIZE * (TOPK + 1) * BLK,
            bytes_accessed=16 << 20,
            transcendentals=half * QUERY_HEADS * (TOPK + 1) * BLK,
        ),
    )(selected.T, queries, stretch_keys, stretch_values, cache_keys, cache_values)


def solution(mesh):
    split = P(("groups", "seq"), None)
    return jax.shard_map(
        per_device,
        mesh=mesh,
        in_specs=(split, split, split, split, split, P("groups", None)),
        out_specs=split,
        check_vma=False,
    )
```

time: 128 us -> 119 us (0.930)
  Pallas kernels: 122 us -> 114 us
  local copies, waits for them, and re-layouts: 4.48 us -> 3.13 us
    pallas_call x1, Pallas kernels: 122 us -> 114 us  [per_device(): pl.pallas_call(functools.partial(kernel, members, holders, relayed), out_...]
    unnamed x2 -> x1, local copies, waits for them, and re-layouts: 4.48 us -> 3.13 us
where the time goes in v2:
time: 119 us; the launch traced here: 118 us
  Pallas kernels  114 us (96%)
  local copies, waits for them, and re-layouts  3.13 us (3%)
    pallas_call x1, Pallas kernels, per_device(): pl.pallas_call(functools.partial(kernel, members, holders, relayed), out_...  114 us
    unnamed x1, local copies, waits for them, and re-layouts  3.13 us

profile of v2, /device:TPU:0, one launch (start us, length us, event | category | flops | bytes accessed | tf_op | source)
XLA Modules:
  0.0 117.6 jit_solution(5173111866909406811)
XLA Ops:
  0.0 114.5 %shard_map.64 = bf16[256,4096]{1,0:T(8,128)(2,1)} custom-call(s32[3,8]{1,0:T(4,128)} %bitcast.1, bf16[256,4096]{1,0:T(8,128)(2,1)} %queries.1, bf16[256,1024]{1,0:T(8,128)(2,1)} %stretch_keys.1, bf16[256,1024]{1,0:T(8,128)(2,1)} %stretch_values.1, bf16[512,1024]{1,0:T(8,128)(2,1)} %cache_keys.1, bf16[512,1024]{1,0:T(8,128)(2,1)} %cache_values.1), custom_call_target="tpu_custom_call" | custom-call | flops 8589934592 | bytes 16777216 | tf_op jit(solution)/shard_map/pallas_call | solution.py:332
  114.5 3.1 %copy.8 = bf16[256,4096]{1,0:T(8,128)(2,1)} copy(bf16[256,4096]{1,0:T(8,128)(2,1)} %shard_map.64) | data formatting | bytes 4194304

commit v3 on v2

--- a/solution.py
+++ b/solution.py
@@ -14,7 +14,6 @@
 TOPK = 3
 CORES = 2
 CHUNKS = KEY_VALUE_HEADS // CORES
-STAGES = 2 * CHUNKS
 SHARE = QUERY_HEADS // KEY_VALUE_HEADS
 WIDE = SHARE * HEAD_SIZE
 SCALE = HEAD_SIZE ** (-0.5) * 1.4426950408889634
@@ -45,23 +44,24 @@
     return weighted(scores, largest, values) + weighted(own, largest, own_values), largest
 
 
-def attend_last(q, keys, values, both, before):
+def attend_later(q, keys, values, both, before):
     scores = product(q, keys)
     largest = jnp.maximum(before, jnp.max(scores, axis=-1, keepdims=True))
     both = both * jnp.exp2((before - largest) * SCALE) + weighted(scores, largest, values)
-    return (both[:, :HEAD_SIZE] / both[:, HEAD_SIZE:]).astype(jnp.bfloat16)
+    return both, largest
 
 
 def kernel(
-    members, holders, relayed,
+    members, holders, relayed, parts,
     selected, queries, stretch_keys, stretch_values, cache_keys, cache_values,
     out,
     *scratch,
 ):
-    held = scratch[:STAGES]
-    staged, packed, kv, own, qs, outs, sums, tops = scratch[STAGES:STAGES + 8]
+    stages = CHUNKS * len(parts)
+    held = scratch[:stages]
+    staged, packed, kv, own, qs, outs, sums, tops = scratch[stages:stages + 8]
     (stage_sem, spread_send, spread_recv, near_recv, relay_send, fetch_send, fetch_recv,
-     own_send, own_recv, q_send, q_recv, o_send, o_recv, o_local) = scratch[STAGES + 8:]
+     own_send, own_recv, q_send, q_recv, o_send, o_recv, o_local) = scratch[stages + 8:]
 
     me = lax.axis_index("seq")
     core = lax.rem(me, CORES)
@@ -80,7 +80,6 @@
         set_size = holders
         base = (me // holders) * holders
     half = queries.shape[0]
-    piece = BLK // (2 * holders)
     my_rows = pl.ds(pl.multiple_of(core * half, half), half)
     other_rows = pl.ds(pl.multiple_of((1 - core) * half, half), half)
 
@@ -103,11 +102,12 @@
     pl.semaphore_wait(barrier, members - 1)
 
     def rows_of(s, holder):
-        first = (s % 2) * (BLK // 2) + holder * piece
-        return pl.ds(pl.multiple_of(first, piece), piece)
+        n = s % len(parts)
+        first = sum(parts[:n]) * holders + holder * parts[n]
+        return pl.ds(pl.multiple_of(first, 16), parts[n])
 
     def spread_near(s):
-        h = s // 2
+        h = s // len(parts)
 
         @pl.loop(0, holders)
         def _(k):
@@ -137,8 +137,8 @@
             ).start()
 
     def spread(s):
-        h = s // 2
-        if s % 2 == 0:
+        h = s // len(parts)
+        if s % len(parts) == 0:
             pltpu.make_async_copy(staged.at[h], staged.at[h], stage_sem.at[h]).wait()
         if relayed:
             spread_near(s)
@@ -190,13 +190,15 @@
                         device_id={"seq": sibling}, device_id_type=MESH,
                     ).start()
 
-    for s in range(2 if relayed else 1, STAGES if not relayed else 3):
+    for s in range(2 if relayed else 1, stages if not relayed else 3):
         spread(s)
 
     def fetch(s):
         arrived = held[s].at[pl.ds(0, set_size)] if relayed else held[s]
         pltpu.make_async_copy(arrived, arrived, spread_recv.at[s]).wait()
+        piece = parts[s % len(parts)]
         land = kv.at[s, :, :, pl.ds(pl.multiple_of(mine * piece, piece), piece), :]
+        kept = pl.ds(0, piece)
 
         here = me - base
 
@@ -206,22 +208,27 @@
             to = base + i
             for t in range(TOPK):
                 block = selected[t, to // CORES]
-                packed[s, i, t] = held[s][block, lax.rem(to, CORES)]
+                packed[s, i, t, :, 0:piece] = held[s][block, lax.rem(to, CORES)]
 
             @pl.when(k == 0)
             def _():
-                pltpu.make_async_copy(packed.at[s, i], land, fetch_recv.at[s]).start()
+                pltpu.make_async_copy(packed.at[s, i, :, :, kept], land, fetch_recv.at[s]).start()
 
             @pl.when(k > 0)
             def _():
                 pltpu.make_async_remote_copy(
-                    src_ref=packed.at[s, i], dst_ref=land,
+                    src_ref=packed.at[s, i, :, :, kept], dst_ref=land,
                     send_sem=fetch_send.at[s], recv_sem=fetch_recv.at[s],
                     device_id={"seq": to}, device_id_type=MESH,
                 ).start()
 
-    def picked(s, n):
-        return kv[s, :, n].reshape(TOPK * BLK // 2, HEAD_SIZE)
+    def picked(s, n, n_part):
+        rows = parts[n_part] * holders
+        return kv[s, :, n, 0:rows].reshape(TOPK * rows, HEAD_SIZE)
+
+    def await_picked(s, n_part):
+        arrived = kv.at[s, :, :, pl.ds(0, parts[n_part] * holders)]
+        pltpu.make_async_copy(arrived, arrived, fetch_recv.at[s]).wait()
 
     def tiles(body):
         @pl.loop(0, SHARE // 2)
@@ -233,15 +240,15 @@
                     body(g, lanes, r, pl.ds(r * half, half))
 
     def first_part(h):
-        s = 2 * h
-        pltpu.make_async_copy(kv.at[s], kv.at[s], fetch_recv.at[s]).wait()
+        s = len(parts) * h
+        await_picked(s, 0)
         pltpu.make_async_copy(own.at[h], own.at[h], own_recv.at[h]).wait()
         pltpu.make_async_copy(qs.at[h], qs.at[h], q_recv.at[h]).wait()
 
         def body(g, lanes, r, rows):
             seen = (r + 1) * half
             both, largest = attend_first(
-                qs[h, rows, lanes], picked(s, 0), picked(s, 1),
+                qs[h, rows, lanes], picked(s, 0, 0), picked(s, 1, 0),
                 own[h, 0, 0:seen], own[h, 1, 0:seen], r * half,
             )
             sums[g, rows] = both
@@ -249,18 +256,27 @@
 
         tiles(body)
 
-    def last_part(h):
-        s = 2 * h + 1
-        pltpu.make_async_copy(kv.at[s], kv.at[s], fetch_recv.at[s]).wait()
+    def later_part(h, n_part):
+        s = len(parts) * h + n_part
+        await_picked(s, n_part)
 
         def body(g, lanes, r, rows):
-            outs[h, rows, lanes] = attend_last(
-                qs[h, rows, lanes], picked(s, 0), picked(s, 1),
+            both, largest = attend_later(
+                qs[h, rows, lanes], picked(s, 0, n_part), picked(s, 1, n_part),
                 sums[g, rows], tops[g, rows][:, :1],
             )
+            if n_part < len(parts) - 1:
+                sums[g, rows] = both
+                tops[g, rows] = jnp.broadcast_to(largest, (half, HEAD_SIZE))
+            else:
+                done = both[:, :HEAD_SIZE] / both[:, HEAD_SIZE:]
+                outs[h, rows, lanes] = done.astype(jnp.bfloat16)
 
         tiles(body)
-
+        if n_part == len(parts) - 1:
+            give_back(h)
+
+    def give_back(h):
         lanes = pl.ds(pl.multiple_of((core * CHUNKS + h) * WIDE, WIDE), WIDE)
         pltpu.make_async_copy(outs.at[h, my_rows, :], out.at[:, lanes], o_local).start()
         pltpu.make_async_remote_copy(
@@ -269,24 +285,27 @@
             device_id={"seq": sibling}, device_id_type=MESH,
         ).start()
 
-    @pl.loop(0, STAGES + 1)
+    @pl.loop(0, stages + 1)
     def _(step):
-        for s in range(STAGES):
+        for s in range(stages):
             @pl.when(step == s)
             def _():
-                if relayed and s + 2 < STAGES:
+                if relayed and s + 2 < stages:
                     holding(relay, s + 2)
-                if relayed and s + 3 < STAGES:
+                if relayed and s + 3 < stages:
                     spread(s + 3)
                 holding(fetch, s)
 
-        @pl.when((step > 0) & (lax.rem(step, 2) == 1))
+        before = step - 1
+
+        @pl.when((step > 0) & (lax.rem(before, len(parts)) == 0))
         def _():
-            first_part((step - 1) // 2)
-
-        @pl.when((step > 0) & (lax.rem(step, 2) == 0))
-        def _():
-            last_part((step - 1) // 2)
+            first_part(before // len(parts))
+
+        for n_part in range(1, len(parts)):
+            @pl.when((step > 0) & (lax.rem(before, len(parts)) == n_part))
+            def _():
+                later_part(before // len(parts), n_part)
 
     def await_sent(count, s):
         sent = held[s].at[pl.ds(0, count)]
@@ -297,10 +316,10 @@
             await_sent(holders - 1, s)
             sent = held[s].at[pl.ds(0, set_size)]
             pltpu.make_async_copy(sent, sent, relay_send.at[s]).wait()
-        sent = packed.at[s, pl.ds(0, set_size - 1)]
+        sent = packed.at[s, pl.ds(0, set_size - 1), :, :, pl.ds(0, parts[s % len(parts)])]
         pltpu.make_async_copy(sent, sent, fetch_send.at[s]).wait()
 
-    for s in range(STAGES):
+    for s in range(stages):
         if relayed:
             pl.when(away == 1)(functools.partial(await_sent, holders, s))
         else:
@@ -325,28 +344,30 @@
     relayed = members == 16
     holders = members // 4 if relayed else min(members // 2, BLK // 32)
     set_size = 2 * holders if relayed else holders
-    piece = BLK // (2 * holders)
+    parts = (BLK // 8, BLK // 16, BLK // 16) if relayed else (BLK // (2 * holders),) * 2
+    stages = CHUNKS * len(parts)
     bf16 = jnp.bfloat16
     dma = pltpu.SemaphoreType.DMA
     anywhere = pl.BlockSpec(memory_space=pl.ANY)
     return pl.pallas_call(
-        functools.partial(kernel, members, holders, relayed),
+        functools.partial(kernel, members, holders, relayed, parts),
         out_shape=jax.ShapeDtypeStruct(queries.shape, bf16),
         in_specs=[pl.BlockSpec(memory_space=pltpu.SMEM)] + [anywhere] * 5,
         out_specs=anywhere,
         scratch_shapes=[
-            pltpu.VMEM((members, CORES, 2, piece, HEAD_SIZE), bf16) for _ in range(STAGES)
+            pltpu.VMEM((members, CORES, 2, parts[s % len(parts)], HEAD_SIZE), bf16)
+            for s in range(stages)
         ] + [
             pltpu.VMEM((CHUNKS, CORES, 2, BLK, HEAD_SIZE), bf16),
-            pltpu.VMEM((STAGES, set_size, TOPK, 2, piece, HEAD_SIZE), bf16),
-            pltpu.VMEM((STAGES, TOPK, 2, BLK // 2, HEAD_SIZE), bf16),
+            pltpu.VMEM((stages, set_size, TOPK, 2, max(parts), HEAD_SIZE), bf16),
+            pltpu.VMEM((stages, TOPK, 2, max(parts) * holders, HEAD_SIZE), bf16),
             pltpu.VMEM((CHUNKS, 2, BLK, HEAD_SIZE), bf16),
             pltpu.VMEM((CHUNKS, BLK, WIDE), bf16),
             pltpu.VMEM((CHUNKS, BLK, WIDE), bf16),
             pltpu.VMEM((SHARE, BLK, 2 * HEAD_SIZE), jnp.float32),
             pltpu.VMEM((SHARE, BLK, HEAD_SIZE), jnp.float32),
-            dma((CHUNKS,)), dma((STAGES,)), dma((STAGES,)), dma((STAGES, 2)), dma((STAGES,)),
-            dma((STAGES,)), dma((STAGES,)),
+            dma((CHUNKS,)), dma((stages,)), dma((stages,)), dma((stages, 2)), dma((stages,)),
+            dma((stages,)), dma((stages,)),
             dma, dma((CHUNKS,)), dma, dma((CHUNKS,)), dma, dma, dma,
         ],
         compiler_params=pltpu.CompilerParams(

time: 119 us -> 117 us (0.983); the launches traced: 118 us -> 117 us
  no operation moved by 1% of the time
where the time goes in v3:
time: 117 us
  Pallas kernels  114 us (97%)
  local copies, waits for them, and re-layouts  3.13 us (3%)
    pallas_call x1, Pallas kernels, per_device(): pl.pallas_call(functools.partial(kernel, members, holders, relayed, parts...  114 us
    unnamed x1, local copies, waits for them, and re-layouts  3.13 us

profile of v3, /device:TPU:0, one launch (start us, length us, event | category | flops | bytes accessed | tf_op | source)
XLA Modules:
  0.0 117.3 jit_solution(6140756522666906535)
XLA Ops:
  0.0 114.2 %shard_map.64 = bf16[256,4096]{1,0:T(8,128)(2,1)} custom-call(s32[3,8]{1,0:T(4,128)} %bitcast.1, bf16[256,4096]{1,0:T(8,128)(2,1)} %queries.1, bf16[256,1024]{1,0:T(8,128)(2,1)} %stretch_keys.1, bf16[256,1024]{1,0:T(8,128)(2,1)} %stretch_values.1, bf16[512,1024]{1,0:T(8,128)(2,1)} %cache_keys.1, bf16[512,1024]{1,0:T(8,128)(2,1)} %cache_values.1), custom_call_target="tpu_custom_call" | custom-call | flops 8589934592 | bytes 16777216 | tf_op jit(solution)/shard_map/pallas_call | solution.py:352
  114.2 3.1 %copy.8 = bf16[256,4096]{1,0:T(8,128)(2,1)} copy(bf16[256,4096]{1,0:T(8,128)(2,1)} %shard_map.64) | data formatting | bytes 4194304

commit v4 on v3

--- a/solution.py
+++ b/solution.py
@@ -344,7 +344,7 @@
     relayed = members == 16
     holders = members // 4 if relayed else min(members // 2, BLK // 32)
     set_size = 2 * holders if relayed else holders
-    parts = (BLK // 8, BLK // 16, BLK // 16) if relayed else (BLK // (2 * holders),) * 2
+    parts = (BLK // 16,) * 4 if relayed else (BLK // (2 * holders),) * 2
     stages = CHUNKS * len(parts)
     bf16 = jnp.bfloat16
     dma = pltpu.SemaphoreType.DMA

time: 117 us -> 115 us (0.983)
  Pallas kernels: 114 us -> 111 us
    pallas_call x1, Pallas kernels: 114 us -> 111 us  [per_device(): pl.pallas_call(functools.partial(kernel, members, holders, relayed, parts...]
where the time goes in v4:
time: 115 us; the launch traced here: 114 us
  Pallas kernels  111 us (97%)
  local copies, waits for them, and re-layouts  3.13 us (3%)
    pallas_call x1, Pallas kernels, per_device(): pl.pallas_call(functools.partial(kernel, members, holders, relayed, parts...  111 us
    unnamed x1, local copies, waits for them, and re-layouts  3.13 us

profile of v4, /device:TPU:0, one launch (start us, length us, event | category | flops | bytes accessed | tf_op | source)
XLA Modules:
  0.0 114.3 jit_solution(9511024919075461628)
XLA Ops:
  0.0 111.2 %shard_map.64 = bf16[256,4096]{1,0:T(8,128)(2,1)} custom-call(s32[3,8]{1,0:T(4,128)} %bitcast.1, bf16[256,4096]{1,0:T(8,128)(2,1)} %queries.1, bf16[256,1024]{1,0:T(8,128)(2,1)} %stretch_keys.1, bf16[256,1024]{1,0:T(8,128)(2,1)} %stretch_values.1, bf16[512,1024]{1,0:T(8,128)(2,1)} %cache_keys.1, bf16[512,1024]{1,0:T(8,128)(2,1)} %cache_values.1), custom_call_target="tpu_custom_call" | custom-call | flops 8589934592 | bytes 16777216 | tf_op jit(solution)/shard_map/pallas_call | solution.py:352
  111.2 3.1 %copy.8 = bf16[256,4096]{1,0:T(8,128)(2,1)} copy(bf16[256,4096]{1,0:T(8,128)(2,1)} %shard_map.64) | data formatting | bytes 4194304
